TPU v7x, 32 devices: a whole 2x2x4 slice. The times are simulated.
32 devices in a mesh: groups: 2 (over x), out: 8 (over z, y), in: 2 (over core).
Axes of the slice: x: 2, y: 2, z: 4, core: 2. Of those that a mesh axis runs over, the one named last changes fastest.
Arguments:
- features: bfloat16 [512, 16384], P(('groups', 'out'), 'in'), parts along dimension 0, may hold values from -6 to 6
- weight: bfloat16 [16384, 16384], P('in', 'out'), may hold values from -0.046875 to 0.046875
- grad_output: bfloat16 [512, 16384], P(('groups', 'in'), 'out'), parts along dimension 0, may hold values from -0.375 to 0.375
Outputs:
- activation: bfloat16 [512, 16384], P(('groups', 'in'), 'out'), parts along dimension 0
- grad_input: bfloat16 [512, 16384], P(('groups', 'out'), 'in'), parts along dimension 0
- grad_weight: bfloat16 [32768, 16384], P(('groups', 'in'), 'out'), parts along dimension 0
There are 2 independent parts, one for each index of `groups`. A program takes and returns all parts, laid end to end along the dimension named above; an argument that names none is the same for every part. Nothing has to cross between parts.
All inputs are finite; a program needn't handle non-finite values.
Results may differ from a plain program's by a relative error of at most 0.005.
Values may be sent and summed in bfloat16 or wider, within the bound.
A program may use at most 192 MiB of HBM per device.

v0:
```python
import jax
import jax.numpy as jnp
from jax import lax
from jax.sharding import PartitionSpec as P


def grad_of(cotangent, pre):
    sig = jax.nn.sigmoid(pre)
    return (cotangent.astype(jnp.float32) * sig * (1.0 + pre * (1.0 - sig))).astype(jnp.bfloat16)


def shards(features, weight, grad_output):
    all_inputs = lax.all_gather(features, "out", axis=0, tiled=True)
    pre_part = jnp.dot(all_inputs, weight, preferred_element_type=jnp.float32)
    own_pre = lax.psum_scatter(pre_part, "in", scatter_dimension=0, tiled=True)
    activation = jax.nn.silu(own_pre).astype(jnp.bfloat16)
    grad_pre = lax.all_gather(grad_of(grad_output, own_pre), "in", axis=0, tiled=True)
    grad_input = lax.psum_scatter(
        lax.dot_general(
            grad_pre, weight, (((1,), (1,)), ((), ())), preferred_element_type=jnp.float32
        ),
        "out",
        scatter_dimension=0,
        tiled=True,
    ).astype(jnp.bfloat16)
    grad_weight = lax.dot_general(
        all_inputs, grad_pre, (((0,), (0,)), ((), ())), preferred_element_type=jnp.float32
    ).astype(jnp.bfloat16)
    return (activation, grad_input, grad_weight)


def solution(mesh):
    in_specs = (P(("groups", "out"), "in"), P("in", "out"), P(("groups", "in"), "out"))
    out_specs = (P(("groups", "in"), "out"), P(("groups", "out"), "in"), P(("groups", "in"), "out"))
    return jax.shard_map(shards, mesh=mesh, in_specs=in_specs, out_specs=out_specs, check_vma=False)
```

profile of v0, /device:TPU:0, one launch (start us, length us, event | category | flops | bytes accessed | tf_op | source)
XLA Modules:
  0.0 305.1 jit_solution(202862780982847547)
XLA Ops:
  7.2 0.0 copy-start.1
  7.2 0.0 all-gather.3.cloned.1.call-start
  7.2 0.7 all-gather.3.cloned.1.call-update
  7.9 0.0 reduce-scatter.3.cloned.1.call-start
  8.0 78.3 %all-gather.3.cloned.1.call-done = bf16[256,8192]{1,0:T(8,128)(2,1)} async-done(((bf16[32,8192]{1,0:T(8,128)(2,1)}), bf16[256,8192]{1,0:T(8,128)(2,1)}) %all-gather.3.cloned.1.call-update) | async-done | bytes 4194320 | tf_op jit(solution)/shard_map/all_gather | solution.py:13
  86.3 17.2 %fusion = f32[256,2048]{1,0:T(8,128)} fusion(bf16[256,8192]{1,0:T(8,128)(2,1)} %all-gather.3.cloned.1.call-done, bf16[8192,2048]{1,0:T(8,128)(2,1)} %param.4), kind=kOutput, calls=%fused_computation.4 | convolution fusion | flops 8589934592 | bytes 39845888 | tf_op jit(solution)/shard_map/dot_general | solution.py:14
  103.5 0.0 reduce-scatter.3.cloned.1.call-update
  103.5 0.0 all-gather.5.cloned.1.call-start
  103.5 8.0 %reduce-scatter.3.cloned.1.call-done = f32[128,2048]{1,0:T(8,128)} async-done(((f32[256,2048]{1,0:T(8,128)}), f32[128,2048]{1,0:T(8,128)}) %reduce-scatter.3.cloned.1.call-update) | async-done | bytes 1048592 | tf_op jit(solution)/shard_map/reduce_scatter | solution.py:15
  111.5 0.0 copy-done.1
  111.5 2.7 multiply_convert_fusion
  114.1 0.0 all-gather.5.cloned.1.call-update
  114.2 0.0 reduce-scatter.5.cloned.1.call-start
  114.2 10.3 %all-gather.5.cloned.1.call-done = bf16[256,2048]{1,0:T(8,128)(2,1)} async-done(((bf16[128,2048]{1,0:T(8,128)(2,1)}), bf16[256,2048]{1,0:T(8,128)(2,1)}) %all-gather.5.cloned.1.call-update) | async-done | bytes 1048592 | tf_op jit(solution)/shard_map/all_gather | solution.py:17
  124.6 0.0 copy-start
  124.6 21.6 %fusion.1 = f32[256,8192]{1,0:T(8,128)} fusion(bf16[256,2048]{1,0:T(8,128)(2,1)} %all-gather.5.cloned.1.call-done, bf16[8192,2048]{1,0:T(8,128)(2,1)} %param.4), kind=kOutput, calls=%fused_computation.5 | convolution fusion | flops 8589934592 | bytes 42991616 | tf_op jit(solution)/shard_map/dot_general | solution.py:19
  146.1 0.0 reduce-scatter.5.cloned.1.call-update
  146.2 0.0 copy-done
  146.2 16.3 %convert_bitcast_fusion = bf16[8192,2048]{0,1:T(8,128)(2,1)} fusion(bf16[256,2048]{1,0:T(8,128)(2,1)S(1)} %copy-done, bf16[256,8192]{1,0:T(8,128)(2,1)} %all-gather.3.cloned.1.call-done), kind=kOutput, calls=%fused_computation | convolution fusion | flops 8606711808 | bytes 38797312 | tf_op jit(solution)/shard_map/dot_general | solution.py:26
  162.4 44.4 %copy.6 = bf16[8192,2048]{1,0:T(8,128)(2,1)} copy(bf16[8192,2048]{0,1:T(8,128)(2,1)} %convert_bitcast_fusion) | data formatting | bytes 67108864
  206.8 89.6 %reduce-scatter.5.cloned.1.call-done = f32[32,8192]{1,0:T(8,128)} async-done(((f32[256,8192]{1,0:T(8,128)}), f32[32,8192]{1,0:T(8,128)}) %reduce-scatter.5.cloned.1.call-update) | async-done | bytes 1048592 | tf_op jit(solution)/shard_map/reduce_scatter | solution.py:18
  296.5 2.1 convert_element_type.21
Async XLA Ops:
  7.2 104.3 %copy-start.1 = (bf16[128,2048]{1,0:T(8,128)(2,1)S(1)}, bf16[128,2048]{1,0:T(8,128)(2,1)}, u32[]{:S(2)}) copy-start(bf16[128,2048]{1,0:T(8,128)(2,1)} %param.5) | copy-start | bytes 1572868
  7.2 79.1 %all-gather.3.cloned.1.call-start = ((), (), s32[]{:S(2)}) async-start(), calls=%async_computation.2 | async-start | bytes 4718592 | tf_op jit(solution)/shard_map/all_gather | solution.py:13
  7.9 103.6 %reduce-scatter.3.cloned.1.call-start = ((), (), s32[]{:S(2)}) async-start(), calls=%async_computation.3 | async-start | bytes 3145728 | tf_op jit(solution)/shard_map/reduce_scatter | solution.py:15
  103.5 21.1 %all-gather.5.cloned.1.call-start = ((), (), s32[]{:S(2)}) async-start(), calls=%async_computation.4 | async-start | bytes 1572864 | tf_op jit(solution)/shard_map/all_gather | solution.py:17
  114.2 182.3 %reduce-scatter.5.cloned.1.call-start = ((), (), s32[]{:S(2)}) async-start(), calls=%async_computation.5 | async-start | bytes 9437184 | tf_op jit(solution)/shard_map/reduce_scatter | solution.py:18
  124.6 21.6 %copy-start = (bf16[256,2048]{1,0:T(8,128)(2,1)S(1)}, bf16[256,2048]{1,0:T(8,128)(2,1)}, u32[]{:S(2)}) copy-start(bf16[256,2048]{1,0:T(8,128)(2,1)} %all-gather.5.cloned.1.call-done) | copy-start | bytes 3145732
Sparse Core Ops, SparseCore 0:
  10.1 76.0 all-gather.2
  103.6 7.8 reduce-scatter.2
  114.3 10.2 all-gather.4
  146.3 150.1 reduce-scatter.4
where the time goes:
time: 306 us; the launch traced here: 305 us
  waiting for transfers between devices  187 us (61%)
  matrix products  55 us (18%)
  local copies, waits for them, and re-layouts  44.4 us (15%)
  between operations  13.8 us (5%)
  other arithmetic  4.72 us (2%)
    reduce_scatter x1, waiting for transfers between devices, shards(): lax.psum_scatter(lax.dot_general(grad_pre, weight, (((1,), (1,)), ((), ()...  89.6 us
    all_gather x1, waiting for transfers between devices, shards(): all_inputs = lax.all_gather(features, 'out', axis=0, tiled=True)  78.3 us
    unnamed x5, local copies, waits for them, and re-layouts  44.4 us
    dot_general x1, matrix products, shards(): lax.dot_general(grad_pre, weight, (((1,), (1,)), ((), ())), preferred_ele...  21.6 us
    dot_general x1, matrix products, shards(): pre_part = jnp.dot(all_inputs, weight, preferred_element_type=jnp.float32)  17.2 us
    dot_general x1, matrix products, shards(): lax.dot_general(all_inputs, grad_pre, (((0,), (0,)), ((), ())), preferred...  16.3 us
    all_gather x1, waiting for transfers between devices, shards(): lax.all_gather(grad_of(grad_output, own_pre), 'in', axis=0, tiled=True)  10.3 us
    reduce_scatter x1, waiting for transfers between devices, shards(): own_pre = lax.psum_scatter(pre_part, 'in', scatter_dimension=0, tiled=True)  7.96 us
  transfers between devices with their start and end apart: 4, of which 4 were waited for; matrix products, arithmetic and copies ran while one was open for 20% of the time, Pallas kernels for 0%

commit v1 on v0

v1 whole, which is shorter than its diff:
```python
import functools

import jax
import jax.numpy as jnp
from jax import lax
from jax.experimental import pallas as pl
from jax.experimental.pallas import tpu as pltpu
from jax.sharding import PartitionSpec as P

MESH = pl.DeviceIdType.MESH
CHUNKS = 8
F32 = jnp.float32
BF16 = jnp.bfloat16


def layer_kernel(
    nz, ny, chunks,
    x_ref, w_ref, g_ref,
    act_ref, gi_ref, xall_out, gp_out,
    xall, w, acc, theirs, gp, keep, ysend, yrecv, zsend, zrecv,
    w_sem, x_sem, out_sem,
    zs, zr, ys, yr, ps, pr, gs, gr, rys, ryr, rzs, rzr,
):
    n, rows, depth = xall.shape
    width = w.shape[1]
    batch = n * rows
    half = batch // 2
    cc = depth // chunks
    nt = min(512, width)
    tiles = width // nt
    me = lax.axis_index("out")
    z, y = me // ny, lax.rem(me, ny)
    core = lax.axis_index("in")
    other_y = z * ny + (1 - y)
    other_core = 1 - core

    def ahead(d):
        return lax.rem(z + d, nz)

    def behind(d):
        return lax.rem(z + nz - d, nz)

    def cols(k):
        return pl.ds(pl.multiple_of(k * cc, cc), cc)

    def tile(j):
        return pl.ds(pl.multiple_of(j * nt, nt), nt)

    def to_out(src, dst, send, recv, peer):
        return pltpu.make_async_remote_copy(
            src_ref=src, dst_ref=dst, send_sem=send, recv_sem=recv,
            device_id={"out": peer}, device_id_type=MESH)

    def to_core(src, dst, send, recv):
        return pltpu.make_async_remote_copy(
            src_ref=src, dst_ref=dst, send_sem=send, recv_sem=recv,
            device_id={"in": other_core}, device_id_type=MESH)

    def w_copy(k):
        return pltpu.make_async_copy(w_ref.at[cols(k), :], w.at[cols(k), :], w_sem.at[k])

    own_copy = pltpu.make_async_copy(x_ref, xall.at[me], x_sem.at[0])
    own_copy.start()

    barrier = pltpu.get_barrier_semaphore()
    for d in range(1, nz):
        pl.semaphore_signal(barrier, inc=1, device_id={"out": ahead(d) * ny + y}, device_id_type=MESH)
    pl.semaphore_signal(barrier, inc=1, device_id={"out": other_y}, device_id_type=MESH)
    pl.semaphore_signal(barrier, inc=1, device_id={"in": other_core}, device_id_type=MESH)
    pl.semaphore_wait(barrier, nz + 1)

    def z_copy(k, d, slot):
        return to_out(x_ref.at[:, cols(k)], xall.at[slot, :, cols(k)], zs.at[k, d - 1], zr.at[k, d - 1], ahead(d) * ny + y)

    def y_own(k, slot):
        return to_out(x_ref.at[:, cols(k)], xall.at[slot, :, cols(k)], ys.at[k, 0], yr.at[k, 0], other_y)

    def y_pass(k, d, slot):
        return to_out(xall.at[slot, :, cols(k)], xall.at[slot, :, cols(k)], ys.at[k, d], yr.at[k, d], other_y)

    @pl.loop(0, chunks)
    def _(k):
        for d in range(1, nz):
            z_copy(k, d, me).start()
        y_own(k, me).start()

    @pl.loop(0, chunks)
    def _(k):
        w_copy(k).start()

    acc[...] = jnp.zeros_like(acc)
    own_copy.wait()

    def forward(k):
        for d in range(1, nz):
            slot = behind(d) * ny + y
            z_copy(k, d, slot).wait_recv()
            y_pass(k, d, slot).start()

    def arrive(k):
        y_own(k, other_y).wait_recv()
        for d in range(1, nz):
            y_pass(k, d, behind(d) * ny + (1 - y)).wait_recv()
        w_copy(k).wait()

    def multiply(k, j):
        acc[:, tile(j)] += jnp.dot(
            xall[:, :, cols(k)].reshape(batch, cc), w[cols(k), tile(j)], preferred_element_type=F32)

    forward(0)

    @pl.loop(1, chunks)
    def _(k):
        forward(k)
        arrive(k - 1)

        @pl.loop(0, tiles)
        def _(j):
            multiply(k - 1, j)

    own_rows = pl.ds(pl.multiple_of(core * half, half), half)
    other_rows = pl.ds(pl.multiple_of(other_core * half, half), half)

    def pre_copy(j):
        return to_core(acc.at[other_rows, tile(j)], theirs.at[:, tile(j)], ps.at[j], pr.at[j])

    def gp_copy(j, where):
        return to_core(gp.at[where, tile(j)], gp.at[where, tile(j)], gs.at[j], gr.at[j])

    arrive(chunks - 1)

    @pl.loop(0, tiles)
    def _(j):
        multiply(chunks - 1, j)
        pre_copy(j).start()

    xall_copy = pltpu.make_async_copy(xall, xall_out, out_sem.at[0])
    xall_copy.start()

    @pl.loop(0, tiles)
    def _(j):
        pre_copy(j).wait_recv()
        pre = acc[own_rows, tile(j)] + theirs[:, tile(j)]
        sig = 1.0 / (1.0 + jnp.exp(-pre))
        act_ref[:, tile(j)] = (pre * sig).astype(BF16)
        gp[own_rows, tile(j)] = (g_ref[:, tile(j)].astype(F32) * sig * (1.0 + pre * (1.0 - sig))).astype(BF16)
        gp_copy(j, own_rows).start()

    @pl.loop(0, tiles)
    def _(j):
        gp_copy(j, other_rows).wait_recv()

    gp_out_copy = pltpu.make_async_copy(gp, gp_out, out_sem.at[1])
    gp_out_copy.start()

    def y_sum(k):
        return to_out(ysend.at[:, :, cols(k)], yrecv.at[:, :, cols(k)], rys.at[k], ryr.at[k], other_y)

    def z_sum(k, d):
        return to_out(zsend.at[ahead(d), :, cols(k)], zrecv.at[d - 1, :, cols(k)], rzs.at[k, d - 1], rzr.at[k, d - 1], ahead(d) * ny + y)

    step = min(512, cc)

    def partial(k):
        @pl.loop(0, cc // step)
        def _(i):
            at = pl.ds(pl.multiple_of(k * cc + i * step, step), step)
            part = lax.dot_general(
                gp[...], w[at, :], (((1,), (1,)), ((), ())), preferred_element_type=F32
            ).reshape(nz, ny, rows, step)
            keep[:, :, at] = jnp.where(y == 0, part[:, 0], part[:, 1])
            ysend[:, :, at] = jnp.where(y == 0, part[:, 1], part[:, 0]).astype(BF16)

        y_sum(k).start()

    def combine(k):
        y_sum(k).wait_recv()
        total = keep[:, :, cols(k)] + yrecv[:, :, cols(k)].astype(F32)
        keep[:, :, cols(k)] = total
        zsend[:, :, cols(k)] = total.astype(BF16)
        for d in range(1, nz):
            z_sum(k, d).start()

    def finish(k):
        total = keep[z, :, cols(k)]
        for d in range(1, nz):
            z_sum(k, d).wait_recv()
            total = total + zrecv[d - 1, :, cols(k)].astype(F32)
        gi_ref[:, cols(k)] = total.astype(BF16)

    @pl.loop(0, chunks + 2)
    def _(k):
        @pl.when(k < chunks)
        def _():
            partial(k)

        @pl.when(k >= 2)
        def _():
            combine(k - 2)

    @pl.loop(0, chunks)
    def _(k):
        finish(k)

    @pl.loop(0, chunks)
    def _(k):
        for d in range(1, nz):
            z_copy(k, d, me).wait_send()
            y_pass(k, d, behind(d) * ny + y).wait_send()
            z_sum(k, d).wait_send()
        y_own(k, me).wait_send()
        y_sum(k).wait_send()

    @pl.loop(0, tiles)
    def _(j):
        pre_copy(j).wait_send()
        gp_copy(j, own_rows).wait_send()

    xall_copy.wait()
    gp_out_copy.wait()


def outer_kernel(x_ref, gp_ref, out_ref):
    width = gp_ref.shape[1]
    nt = min(512, width)

    @pl.loop(0, width // nt)
    def _(j):
        at = pl.ds(pl.multiple_of(j * nt, nt), nt)
        out_ref[:, at] = lax.dot_general(
            x_ref[...], gp_ref[:, at], (((0,), (0,)), ((), ())), preferred_element_type=F32
        ).astype(BF16)


def solution(mesh):
    n = mesh.shape["out"]
    ny = 2
    nz = n // ny

    def shards(features, weight, grad_output):
        rows, depth = features.shape
        width = weight.shape[1]
        batch = n * rows
        half = batch // 2
        chunks = CHUNKS
        tiles = width // min(512, width)
        dma = pltpu.SemaphoreType.DMA
        hbm = pl.BlockSpec(memory_space=pl.ANY)
        vmem = pl.BlockSpec(memory_space=pltpu.VMEM)
        activation, grad_input, all_inputs, grad_pre = pl.pallas_call(
            functools.partial(layer_kernel, nz, ny, chunks),
            out_shape=(
                jax.ShapeDtypeStruct((half, width), BF16),
                jax.ShapeDtypeStruct((rows, depth), BF16),
                jax.ShapeDtypeStruct((n, rows, depth), BF16),
                jax.ShapeDtypeStruct((batch, width), BF16),
            ),
            in_specs=[hbm, hbm, vmem],
            out_specs=(vmem, vmem, hbm, hbm),
            scratch_shapes=[
                pltpu.VMEM((n, rows, depth), BF16),
                pltpu.VMEM((depth, width), BF16),
                pltpu.VMEM((batch, width), F32),
                pltpu.VMEM((half, width), F32),
                pltpu.VMEM((batch, width), BF16),
                pltpu.VMEM((nz, rows, depth), F32),
                pltpu.VMEM((nz, rows, depth), BF16),
                pltpu.VMEM((nz, rows, depth), BF16),
                pltpu.VMEM((nz, rows, depth), BF16),
                pltpu.VMEM((nz - 1, rows, depth), BF16),
                dma((chunks,)), dma((1,)), dma((2,)),
                dma((chunks, nz - 1)), dma((chunks, nz - 1)),
                dma((chunks, nz)), dma((chunks, nz)),
                dma((tiles,)), dma((tiles,)), dma((tiles,)), dma((tiles,)),
                dma((chunks,)), dma((chunks,)),
                dma((chunks, nz - 1)), dma((chunks, nz - 1)),
            ],
            compiler_params=pltpu.CompilerParams(
                collective_id=0, has_side_effects=True, vmem_limit_bytes=62 * 2**20),
            cost_estimate=pl.CostEstimate(
                flops=4 * batch * depth * width, bytes_accessed=2 * depth * width, transcendentals=half * width),
            name="layer",
        )(features, weight, grad_output)
        block = min(512, depth)
        grad_weight = pl.pallas_call(
            outer_kernel,
            out_shape=jax.ShapeDtypeStruct((depth, width), BF16),
            grid=(depth // block,),
            in_specs=[
                pl.BlockSpec((batch, block), lambda i: (0, i)),
                pl.BlockSpec((batch, width), lambda i: (0, 0)),
            ],
            out_specs=pl.BlockSpec((block, width), lambda i: (i, 0)),
            compiler_params=pltpu.CompilerParams(vmem_limit_bytes=40 * 2**20),
            cost_estimate=pl.CostEstimate(
                flops=2 * batch * depth * width, bytes_accessed=2 * depth * width, transcendentals=0),
            name="outer",
        )(all_inputs.reshape(batch, depth), grad_pre)
        return activation, grad_input, grad_weight

    in_specs = (P(("groups", "out"), "in"), P("in", "out"), P(("groups", "in"), "out"))
    out_specs = (P(("groups", "in"), "out"), P(("groups", "out"), "in"), P(("groups", "in"), "out"))
    return jax.shard_map(shards, mesh=mesh, in_specs=in_specs, out_specs=out_specs, check_vma=False)
```

time: 306 us -> 152 us (0.50)
  waiting for transfers between devices: 187 us -> 0 us
  Pallas kernels: 0 us -> 146 us
  matrix products: 55 us -> 0 us
  local copies, waits for them, and re-layouts: 44.4 us -> 5 us
  between operations: 13.8 us -> 0.65 us
  other arithmetic: 4.72 us -> 0 us
    pallas_call x0 -> x2, Pallas kernels: none -> 146 us  [the longest x1 124 us: shards(): pl.pallas_call(functools.partial(layer_kernel, nz, ny, chunks), out_shape...]
    reduce_scatter x2 -> x0, waiting for transfers between devices: 97.6 us -> none  [the longest x1 89.6 us: shards(): lax.psum_scatter(lax.dot_general(grad_pre, weight, (((1,), (1,)), ((), ()...]
    all_gather x2 -> x0, waiting for transfers between devices: 88.6 us -> none  [the longest x1 78.3 us: shards(): all_inputs = lax.all_gather(features, 'out', axis=0, tiled=True)]
    dot_general x3 -> x0, matrix products: 55 us -> none  [the longest x1 21.6 us: shards(): lax.dot_general(grad_pre, weight, (((1,), (1,)), ((), ())), preferred_ele...]
    unnamed x5 -> x10, local copies, waits for them, and re-layouts: 44.4 us -> 5 us
    convert_element_type x2 -> x0, other arithmetic: 4.72 us -> none  [the longest x1 2.65 us: grad_of(): (cotangent.astype(jnp.float32) * sig * (1.0 + pre * (1.0 - sig))).astype(...]
  transfers between devices with their start and end apart: 4 -> 0, of which waited for: 4 -> 0; matrix products, arithmetic and copies ran while one was open for 20% -> 0% of each run, Pallas kernels for 0% -> 0%
where the time goes in v1:
time: 152 us
  Pallas kernels  146 us (96%)
  local copies, waits for them, and re-layouts  5 us (3%)
    pallas_call x1, Pallas kernels, shards(): pl.pallas_call(functools.partial(layer_kernel, nz, ny, chunks), out_shape...  124 us
    pallas_call x1, Pallas kernels, shards(): pl.pallas_call(outer_kernel, out_shape=jax.ShapeDtypeStruct((depth, width...  22.6 us
    unnamed x10, local copies, waits for them, and re-layouts  5 us

profile of v1, /device:TPU:0, one launch (start us, length us, event | category | flops | bytes accessed | tf_op | source)
XLA Modules:
  0.0 151.8 jit_solution(448464493267514740)
XLA Ops:
  0.6 123.5 %layer.1 = (bf16[128,2048]{1,0:T(8,128)(2,1)}, bf16[32,8192]{1,0:T(8,128)(2,1)}, bf16[8,32,8192]{2,1,0:T(8,128)(2,1)}, bf16[256,2048]{1,0:T(8,128)(2,1)}) custom-call(bf16[32,8192]{1,0:T(8,128)(2,1)} %x_ref.1, bf16[8192,2048]{1,0:T(8,128)(2,1)} %w_ref.1, bf16[128,2048]{1,0:T(8,128)(2,1)} %g_ref.1), custom_call_target="tpu_custom_call" | custom-call | flops 17179869184 | bytes 33554432 | tf_op jit(solution)/shard_map/layer/pallas_call | solution.py:250
  124.2 0.0 copy-start
  124.2 2.2 %copy-done = bf16[8,32,8192]{2,1,0:T(8,128)(2,1)S(1)} copy-done((bf16[8,32,8192]{2,1,0:T(8,128)(2,1)S(1)}, bf16[8,32,8192]{2,1,0:T(8,128)(2,1)}, u32[]{:S(2)}) %copy-start) | copy-done | bytes 4194328
  126.4 0.0 copy-start.1
  126.4 1.2 copy-done.1
  127.6 0.0 copy-start.3
  127.6 0.0 copy-start.2
  127.6 22.6 %outer.1 = bf16[8192,2048]{1,0:T(8,128)(2,1)} custom-call(bf16[256,8192]{1,0:T(8,128)(2,1)S(1)} %bitcast.1, bf16[256,2048]{1,0:T(8,128)(2,1)S(1)} %copy-done.1), custom_call_target="tpu_custom_call" | custom-call | flops 8589934592 | bytes 33554432 | tf_op jit(solution)/shard_map/outer/pallas_call | solution.py:285
  150.2 0.0 copy-done.3
  150.2 0.8 copy.8
  151.0 0.0 copy-done.2
  151.0 0.8 copy.9
Async XLA Ops:
  124.2 2.2 %copy-start = (bf16[8,32,8192]{2,1,0:T(8,128)(2,1)S(1)}, bf16[8,32,8192]{2,1,0:T(8,128)(2,1)}, u32[]{:S(2)}) copy-start(bf16[8,32,8192]{2,1,0:T(8,128)(2,1)} %get-tuple-element.9) | copy-start | bytes 12582916
  126.4 1.2 copy-start.1
  127.6 22.6 %copy-start.3 = (bf16[128,2048]{1,0:T(8,128)(2,1)S(1)}, bf16[128,2048]{1,0:T(8,128)(2,1)}, u32[]{:S(2)}) copy-start(bf16[128,2048]{1,0:T(8,128)(2,1)} %get-tuple-element.14) | copy-start | bytes 1572868
  127.6 23.4 %copy-start.2 = (bf16[32,8192]{1,0:T(8,128)(2,1)S(1)}, bf16[32,8192]{1,0:T(8,128)(2,1)}, u32[]{:S(2)}) copy-start(bf16[32,8192]{1,0:T(8,128)(2,1)} %get-tuple-element.15) | copy-start | bytes 1572868

commit v2 on v1

--- a/solution.py
+++ b/solution.py
@@ -9,6 +9,7 @@
 
 MESH = pl.DeviceIdType.MESH
 CHUNKS = 8
+AHEAD = 2
 F32 = jnp.float32
 BF16 = jnp.bfloat16
 
@@ -16,8 +17,8 @@
 def layer_kernel(
     nz, ny, chunks,
     x_ref, w_ref, g_ref,
-    act_ref, gi_ref, xall_out, gp_out,
-    xall, w, acc, theirs, gp, keep, ysend, yrecv, zsend, zrecv,
+    act_ref, gi_ref, xt_out, gp_out,
+    xall, xt, w, acc, theirs, gp, keep, ysend, yrecv, zsend, zrecv,
     w_sem, x_sem, out_sem,
     zs, zr, ys, yr, ps, pr, gs, gr, rys, ryr, rzs, rzr,
 ):
@@ -78,11 +79,14 @@
     def y_pass(k, d, slot):
         return to_out(xall.at[slot, :, cols(k)], xall.at[slot, :, cols(k)], ys.at[k, d], yr.at[k, d], other_y)
 
-    @pl.loop(0, chunks)
-    def _(k):
+    def send(k):
         for d in range(1, nz):
             z_copy(k, d, me).start()
         y_own(k, me).start()
+
+    @pl.loop(0, AHEAD)
+    def _(k):
+        send(k)
 
     @pl.loop(0, chunks)
     def _(k):
@@ -97,17 +101,42 @@
             z_copy(k, d, slot).wait_recv()
             y_pass(k, d, slot).start()
 
+        @pl.when(k + AHEAD < chunks)
+        def _():
+            send(k + AHEAD)
+
     def arrive(k):
         y_own(k, other_y).wait_recv()
         for d in range(1, nz):
             y_pass(k, d, behind(d) * ny + (1 - y)).wait_recv()
         w_copy(k).wait()
+
+    def xt_copy(k):
+        slot = lax.rem(k, 2)
+        return pltpu.make_async_copy(xt.at[slot], xt_out.at[cols(k), :], out_sem.at[slot])
+
+    strip = min(256, cc)
+
+    def turn(k):
+        slot = lax.rem(k, 2)
+
+        @pl.when(k >= 2)
+        def _():
+            xt_copy(k - 2).wait()
+
+        @pl.loop(0, cc // strip)
+        def _(i):
+            at = pl.multiple_of(i * strip, strip)
+            block = xall[:, :, pl.ds(pl.multiple_of(k * cc + at, strip), strip)]
+            xt[slot, pl.ds(at, strip), :] = block.reshape(batch, strip).T
+
+        xt_copy(k).start()
 
     def multiply(k, j):
         acc[:, tile(j)] += jnp.dot(
             xall[:, :, cols(k)].reshape(batch, cc), w[cols(k), tile(j)], preferred_element_type=F32)
 
-    forward(0)
+    forward(jnp.int32(0))
 
     @pl.loop(1, chunks)
     def _(k):
@@ -117,6 +146,8 @@
         @pl.loop(0, tiles)
         def _(j):
             multiply(k - 1, j)
+
+        turn(k - 1)
 
     own_rows = pl.ds(pl.multiple_of(core * half, half), half)
     other_rows = pl.ds(pl.multiple_of(other_core * half, half), half)
@@ -134,8 +165,7 @@
         multiply(chunks - 1, j)
         pre_copy(j).start()
 
-    xall_copy = pltpu.make_async_copy(xall, xall_out, out_sem.at[0])
-    xall_copy.start()
+    turn(jnp.int32(chunks - 1))
 
     @pl.loop(0, tiles)
     def _(j):
@@ -150,7 +180,7 @@
     def _(j):
         gp_copy(j, other_rows).wait_recv()
 
-    gp_out_copy = pltpu.make_async_copy(gp, gp_out, out_sem.at[1])
+    gp_out_copy = pltpu.make_async_copy(gp, gp_out, out_sem.at[2])
     gp_out_copy.start()
 
     def y_sum(k):
@@ -216,20 +246,49 @@
         pre_copy(j).wait_send()
         gp_copy(j, own_rows).wait_send()
 
-    xall_copy.wait()
+    xt_copy(chunks - 2).wait()
+    xt_copy(chunks - 1).wait()
     gp_out_copy.wait()
 
 
-def outer_kernel(x_ref, gp_ref, out_ref):
-    width = gp_ref.shape[1]
+SLOTS = 3
+PARTS = 4
+
+
+def outer_kernel(steps, xt_ref, gp_ref, act_in, gi_in, out_ref, act_ref, gi_ref, held, sems):
+    block, width = held.shape[1:]
     nt = min(512, width)
-
-    @pl.loop(0, width // nt)
-    def _(j):
-        at = pl.ds(pl.multiple_of(j * nt, nt), nt)
-        out_ref[:, at] = lax.dot_general(
-            x_ref[...], gp_ref[:, at], (((0,), (0,)), ((), ())), preferred_element_type=F32
-        ).astype(BF16)
+    part = block // PARTS
+    i = pl.program_id(0)
+    act_ref[...] = act_in[...]
+    gi_ref[...] = gi_in[...]
+
+    def copy(i, p):
+        slot = lax.rem(i, SLOTS)
+        return pltpu.make_async_copy(
+            held.at[slot, pl.ds(p * part, part), :],
+            out_ref.at[pl.ds(pl.multiple_of(i * block + p * part, part), part), :],
+            sems.at[slot, p])
+
+    @pl.when(i >= SLOTS)
+    def _():
+        for p in range(PARTS):
+            copy(i - SLOTS, p).wait()
+
+    slot = lax.rem(i, SLOTS)
+
+    for j in range(width // nt):
+        at = pl.ds(j * nt, nt)
+        held[slot, :, at] = jnp.dot(xt_ref[...], gp_ref[:, at], preferred_element_type=F32).astype(BF16)
+
+    for p in range(PARTS):
+        copy(i, p).start()
+
+    @pl.when(i == steps - 1)
+    def _():
+        for back in range(min(SLOTS, steps)):
+            for p in range(PARTS):
+                copy(steps - 1 - back, p).wait()
 
 
 def solution(mesh):
@@ -247,18 +306,19 @@
         dma = pltpu.SemaphoreType.DMA
         hbm = pl.BlockSpec(memory_space=pl.ANY)
         vmem = pl.BlockSpec(memory_space=pltpu.VMEM)
-        activation, grad_input, all_inputs, grad_pre = pl.pallas_call(
+        activation, grad_input, turned, grad_pre = pl.pallas_call(
             functools.partial(layer_kernel, nz, ny, chunks),
             out_shape=(
                 jax.ShapeDtypeStruct((half, width), BF16),
                 jax.ShapeDtypeStruct((rows, depth), BF16),
-                jax.ShapeDtypeStruct((n, rows, depth), BF16),
+                jax.ShapeDtypeStruct((depth, batch), BF16),
                 jax.ShapeDtypeStruct((batch, width), BF16),
             ),
             in_specs=[hbm, hbm, vmem],
             out_specs=(vmem, vmem, hbm, hbm),
             scratch_shapes=[
                 pltpu.VMEM((n, rows, depth), BF16),
+                pltpu.VMEM((2, depth // chunks, batch), BF16),
                 pltpu.VMEM((depth, width), BF16),
                 pltpu.VMEM((batch, width), F32),
                 pltpu.VMEM((half, width), F32),
@@ -268,7 +328,7 @@
                 pltpu.VMEM((nz, rows, depth), BF16),
                 pltpu.VMEM((nz, rows, depth), BF16),
                 pltpu.VMEM((nz - 1, rows, depth), BF16),
-                dma((chunks,)), dma((1,)), dma((2,)),
+                dma((chunks,)), dma((1,)), dma((3,)),
                 dma((chunks, nz - 1)), dma((chunks, nz - 1)),
                 dma((chunks, nz)), dma((chunks, nz)),
                 dma((tiles,)), dma((tiles,)), dma((tiles,)), dma((tiles,)),
@@ -281,21 +341,32 @@
                 flops=4 * batch * depth * width, bytes_accessed=2 * depth * width, transcendentals=half * width),
             name="layer",
         )(features, weight, grad_output)
-        block = min(512, depth)
-        grad_weight = pl.pallas_call(
-            outer_kernel,
-            out_shape=jax.ShapeDtypeStruct((depth, width), BF16),
-            grid=(depth // block,),
+        block = min(1024, depth // 4)
+        steps = depth // block
+        act_rows = half // min(steps, half // 16)
+        act_spec = pl.BlockSpec((act_rows, width), lambda i: (jnp.minimum(i, half // act_rows - 1), 0))
+        gi_spec = pl.BlockSpec((rows, block), lambda i: (0, i))
+        grad_weight, activation, grad_input = pl.pallas_call(
+            functools.partial(outer_kernel, steps),
+            out_shape=(
+                jax.ShapeDtypeStruct((depth, width), BF16),
+                jax.ShapeDtypeStruct((half, width), BF16),
+                jax.ShapeDtypeStruct((rows, depth), BF16),
+            ),
+            grid=(steps,),
             in_specs=[
-                pl.BlockSpec((batch, block), lambda i: (0, i)),
+                pl.BlockSpec((block, batch), lambda i: (i, 0)),
                 pl.BlockSpec((batch, width), lambda i: (0, 0)),
+                act_spec,
+                gi_spec,
             ],
-            out_specs=pl.BlockSpec((block, width), lambda i: (i, 0)),
-            compiler_params=pltpu.CompilerParams(vmem_limit_bytes=40 * 2**20),
+            out_specs=(hbm, act_spec, gi_spec),
+            scratch_shapes=[pltpu.VMEM((SLOTS, block, width), BF16), dma((SLOTS, PARTS))],
+            compiler_params=pltpu.CompilerParams(vmem_limit_bytes=62 * 2**20),
             cost_estimate=pl.CostEstimate(
                 flops=2 * batch * depth * width, bytes_accessed=2 * depth * width, transcendentals=0),
             name="outer",
-        )(all_inputs.reshape(batch, depth), grad_pre)
+        )(turned, grad_pre, activation, grad_input)
         return activation, grad_input, grad_weight
 
     in_specs = (P(("groups", "out"), "in"), P("in", "out"), P(("groups", "in"), "out"))

time: 152 us -> 140 us (0.921)
  Pallas kernels: 146 us -> 139 us
  local copies, waits for them, and re-layouts: 5 us -> 0 us
    pallas_call x1, Pallas kernels: 22.6 us -> 16.6 us  [shards(): pl.pallas_call(functools.partial(outer_kernel, steps), out_shape=(jax.Sha...]
    unnamed x10 -> x0, local copies, waits for them, and re-layouts: 5 us -> none
where the time goes in v2:
time: 140 us
  Pallas kernels  139 us (99%)
    pallas_call x1, Pallas kernels, shards(): pl.pallas_call(functools.partial(layer_kernel, nz, ny, chunks), out_shape...  123 us
    pallas_call x1, Pallas kernels, shards(): pl.pallas_call(functools.partial(outer_kernel, steps), out_shape=(jax.Sha...  16.6 us

profile of v2, /device:TPU:0, one launch (start us, length us, event | category | flops | bytes accessed | tf_op | source)
XLA Modules:
  0.0 140.0 jit_solution(16918384469600982791)
XLA Ops:
  0.6 122.8 %layer.1 = (bf16[128,2048]{1,0:T(8,128)(2,1)}, bf16[32,8192]{1,0:T(8,128)(2,1)}, bf16[8192,256]{1,0:T(8,128)(2,1)}, bf16[256,2048]{1,0:T(8,128)(2,1)}) custom-call(bf16[32,8192]{1,0:T(8,128)(2,1)} %x_ref.1, bf16[8192,2048]{1,0:T(8,128)(2,1)} %w_ref.1, bf16[128,2048]{1,0:T(8,128)(2,1)} %g_ref.1), custom_call_target="tpu_custom_call" | custom-call | flops 17179869184 | bytes 33554432 | tf_op jit(solution)/shard_map/layer/pallas_call | solution.py:309
  123.4 16.6 %outer.1 = (bf16[8192,2048]{1,0:T(8,128)(2,1)}, bf16[128,2048]{1,0:T(8,128)(2,1)}, bf16[32,8192]{1,0:T(8,128)(2,1)}) custom-call(bf16[8192,256]{1,0:T(8,128)(2,1)} %get-tuple-element.10.xt_ref, bf16[256,2048]{1,0:T(8,128)(2,1)} %get-tuple-element.11.gp_ref, bf16[128,2048]{1,0:T(8,128)(2,1)} %get-tuple-element.12.act_in, bf16[32,8192]{1,0:T(8,128)(2,1)} %get-tuple-element.13.gi_in), custom_call_target="tpu_custom_call" | custom-call | flops 8589934592 | bytes 33554432 | tf_op jit(solution)/shard_map/outer/pallas_call | solution.py:349
